TPU v7x, 32 devices: a whole 2x2x4 slice. The times are simulated.
32 devices in a mesh: dp: 8 (over y, x, core), fsdp: 4 (over z).
Axes of the slice: x: 2, y: 2, z: 4, core: 2. Of those that a mesh axis runs over, the one named last changes fastest.
Arguments:
- grads: bfloat16 [8, 1024, 2048], P('dp', None, 'fsdp'), may hold values from -0.44 to 0.44
- stats: float32 [8, 4, 512, 512], P('dp', 'fsdp'), may hold values from -0.08 to 2, as said below
- left_root: bfloat16 [1024, 2048], P(None, 'fsdp'), may hold values from -0.02 to 1, as said below
- right_root: bfloat16 [1024, 2048], P(None, 'fsdp'), may hold values from -1.25 to 1.25, as said below
- owners: int32 [4, 2], replicated, may hold values from 0 to 7, as said below
Outputs:
- update: bfloat16 [1024, 2048], P(None, 'fsdp')
- new_stats: float32 [8, 4, 512, 512], P('dp', 'fsdp')
- new_root: bfloat16 [1024, 2048], P(None, 'fsdp')
Inputs may be any that keep to these rules, and one draw needn't show every extreme that they name: `stats`: symmetric in each slot. `left_root`: symmetric in each block. `right_root`: symmetric in each block. `owners`: the 2 entries of each row are distinct.
All inputs are finite; a program needn't handle non-finite values.
Results may differ from a plain program's by a relative error of at most 0.033.
Values may be sent and summed in bfloat16 or wider, within the bound.
A program may use at most 64 MiB of HBM per device.

v0:
```python
import jax
import jax.numpy as jnp
from jax import lax
from jax.sharding import PartitionSpec as P

BETA = 0.95
EPSILON = 1e-06


def from_root(array, axis, root):
    mine = lax.axis_index(axis) == root
    return lax.psum(jnp.where(mine, array, jnp.zeros_like(array)), axis)


def precise(left_arg, right_arg):
    return jnp.dot(
        left_arg, right_arg, preferred_element_type=jnp.float32, precision=lax.Precision.HIGHEST
    )


def full_sum(local_grad):
    return lax.psum(local_grad.astype(jnp.float32).astype(jnp.bfloat16), "dp")


def local(grads, stats, left_root, right_root, owners):
    block_width = stats.shape[-1]
    block_rows = left_root.shape[0] // block_width
    replica = lax.axis_index("dp")
    column = lax.axis_index("fsdp")
    owner_row = lax.dynamic_index_in_dim(owners, column, 0, keepdims=False)
    owned_mask = owner_row == replica
    has_block = jnp.any(owned_mask)
    owned_index = jnp.sum(jnp.where(owned_mask, jnp.arange(block_rows, dtype=jnp.int32), 0))
    local_grad = grads[0]
    summed = None
    summed = full_sum(local_grad)
    grad_block = lax.dynamic_slice_in_dim(summed, owned_index * block_width, block_width, 0)
    left_block = lax.dynamic_slice_in_dim(left_root, owned_index * block_width, block_width, 0)
    right_block = lax.dynamic_slice_in_dim(right_root, owned_index * block_width, block_width, 0)
    old_stats = stats[0, 0]

    def fresh_owned():
        outer = lax.dot_general(
            grad_block, grad_block, (((1,), (1,)), ((), ())), preferred_element_type=jnp.float32
        )
        return BETA * old_stats + (1.0 - BETA) * outer

    def fresh_empty():
        return jnp.zeros_like(old_stats)

    fresh_stats = lax.cond(has_block, fresh_owned, fresh_empty)

    def newton_owned():
        start_root = left_block.astype(jnp.float32)
        square = precise(start_root, start_root)
        middle = precise(precise(square, fresh_stats), square)
        identity = jnp.eye(block_width, dtype=jnp.float32)
        return precise(start_root, (5.0 * identity - middle) * 0.25).astype(jnp.bfloat16)

    def newton_empty():
        return jnp.zeros((block_width, block_width), jnp.bfloat16)

    update_pieces = []
    root_pieces = []

    def precondition_owned():
        left_product = jnp.dot(left_block, grad_block, preferred_element_type=jnp.float32).astype(
            jnp.bfloat16
        )
        raw_update = jnp.dot(left_product, right_block, preferred_element_type=jnp.float32)
        return (raw_update.astype(jnp.bfloat16), jnp.sum(raw_update * raw_update))

    def precondition_empty():
        return (jnp.zeros((block_width, block_width), jnp.bfloat16), jnp.zeros((), jnp.float32))

    rounded, squares = lax.cond(has_block, precondition_owned, precondition_empty)
    root_new = lax.cond(has_block, newton_owned, newton_empty)
    for block_index in range(block_rows):
        got_update, got_root = (
            from_root(rounded, "dp", owner_row[block_index]),
            from_root(root_new, "dp", owner_row[block_index]),
        )
        update_pieces.append(got_update)
        root_pieces.append(got_root)
    total_squares = lax.psum(squares, ("dp", "fsdp"))
    rms_scale = lax.rsqrt(
        total_squares / (left_root.shape[0] * block_width * lax.axis_size("fsdp")) + EPSILON
    )
    scaled = [
        (piece.astype(jnp.float32) * rms_scale).astype(jnp.bfloat16) for piece in update_pieces
    ]
    update = jnp.concatenate(scaled, axis=0)
    new_root = jnp.concatenate(root_pieces, axis=0)
    new_stats = fresh_stats[None, None]
    return (update, new_stats, new_root)


def solution(mesh):
    in_specs = (
        P("dp", None, "fsdp"),
        P("dp", "fsdp", None, None),
        P(None, "fsdp"),
        P(None, "fsdp"),
        P(),
    )
    out_specs = (P(None, "fsdp"), P("dp", "fsdp", None, None), P(None, "fsdp"))
    return jax.shard_map(local, mesh=mesh, in_specs=in_specs, out_specs=out_specs, check_vma=False)
```

profile of v0, /device:TPU:0, one launch (start us, length us, event | category | flops | bytes accessed | tf_op | source)
XLA Modules:
  0.0 158.9 jit_solution(9261846464375457204)
XLA Ops:
  7.2 0.0 copy-start
  7.2 0.0 all-reduce.4.cloned.1.call-start
  7.2 0.7 all-reduce.4.cloned.1.call-update
  7.9 0.0 all-reduce.6.cloned.1.call-start
  8.0 0.7 fusion.6
  8.7 0.6 select_reduce_fusion
  10.6 0.5 fusion.8
  12.5 0.0 copy-start.1
  12.5 58.0 %all-reduce.4.cloned.1.call-done = bf16[1024,512]{1,0:T(8,128)(2,1)} async-done(((bf16[1024,512]{1,0:T(8,128)(2,1)}), bf16[1024,512]{1,0:T(8,128)(2,1)}) %all-reduce.4.cloned.1.call-update) | async-done | bytes 1048592 | tf_op jit(solution)/shard_map/psum | solution.py:22
  70.5 1.1 constant_dynamic-slice_fusion
  71.6 1.2 conditional.4
  71.6 1.1 broadcast.25
  72.7 0.1 broadcast_in_dim.8
  72.8 0.0 copy-start.2
  72.9 1.0 copy-done.2
  73.9 0.1 conditional.3
  73.9 1.1 broadcast_select_fusion.2
  75.0 1.0 broadcast_select_fusion.3
  76.0 0.0 all-reduce.6.cloned.1.call-update
  76.1 51.8 %psum.44 = f32[]{:T(128)} all-reduce(f32[]{:T(128)} %get-tuple-element.48), channel_id=1, replica_groups=mesh['dp'=8,'fsdp'=4] {'dp','fsdp'}, use_global_device_ids=true, to_apply=%region_7.8 | all-reduce | flops 1 | bytes 8 | tf_op jit(solution)/shard_map/psum | solution.py:85
  128.5 19.9 %all-reduce.6.cloned.1.call-done = (bf16[512,512]{1,0:T(8,128)(2,1)}, bf16[512,512]{1,0:T(8,128)(2,1)}, bf16[512,512]{1,0:T(8,128)(2,1)}, bf16[512,512]{1,0:T(8,128)(2,1)}) async-done(((bf16[512,512]{1,0:T(8,128)(2,1)}, bf16[512,512]{1,0:T(8,128)(2,1)}, bf16[512,512]{1,0:T(8,128)(2,1)}, bf16[512,512]{1,0:T(8,128)(2,1)}), (bf16[512,512]{1,0:T(8,128)(2,1)}, bf16[512,512]{1,0:T(8,128)(2,1)}, ...) | async-done | bytes 2097168 | tf_op jit(solution)/shard_map/psum | solution.py:12
  148.4 2.3 %pad_maximum_fusion.1 = bf16[1024,512]{1,0:T(8,128)(2,1)} fusion(bf16[512,512]{1,0:T(8,128)(2,1)} %get-tuple-element.60, bf16[512,512]{1,0:T(8,128)(2,1)} %get-tuple-element.61), kind=kLoop, calls=%fused_computation.13 | loop fusion | flops 2097152 | bytes 2097152 | tf_op jit(solution)/shard_map/concatenate | solution.py:93
  150.8 0.2 multiply_convert_fusion
  151.0 1.0 pad_maximum_fusion
  (12 shorter events, 0.2 us)
Async XLA Ops:
  7.2 5.3 %copy-start = (bf16[1024,512]{1,0:T(8,128)(2,1)S(1)}, bf16[1024,512]{1,0:T(8,128)(2,1)}, u32[]{:S(2)}) copy-start(bf16[1024,512]{1,0:T(8,128)(2,1)} %param.13) | copy-start | bytes 3145732
  7.2 0.8 copy-start.5
  7.2 63.3 %all-reduce.4.cloned.1.call-start = ((), (), s32[]{:S(2)}) async-start(), calls=%async_computation | async-start | bytes 2097152 | tf_op jit(solution)/shard_map/psum | solution.py:22
  7.9 140.5 %all-reduce.6.cloned.1.call-start = ((), (), s32[]{:S(2)}) async-start(), calls=%async_computation.1 | async-start | bytes 4194304 | tf_op jit(solution)/shard_map/psum | solution.py:12
  12.5 59.1 %copy-start.1 = (f32[1,1,512,512]{3,2,1,0:T(8,128)S(1)}, f32[1,1,512,512]{3,2,1,0:T(8,128)}, u32[]{:S(2)}) copy-start(f32[1,1,512,512]{3,2,1,0:T(8,128)} %param.12) | copy-start | bytes 3145732
  72.8 1.0 copy-start.2
  148.4 2.3 %copy-start.3 = (bf16[512,512]{1,0:T(8,128)(2,1)S(1)}, bf16[512,512]{1,0:T(8,128)(2,1)}, u32[]{:S(2)}) copy-start(bf16[512,512]{1,0:T(8,128)(2,1)} %get-tuple-element.58) | copy-start | bytes 1572868
  148.4 2.3 %copy-start.4 = (bf16[512,512]{1,0:T(8,128)(2,1)S(1)}, bf16[512,512]{1,0:T(8,128)(2,1)}, u32[]{:S(2)}) copy-start(bf16[512,512]{1,0:T(8,128)(2,1)} %get-tuple-element.59) | copy-start | bytes 1572868
Sparse Core Ops, SparseCore 0:
  11.2 59.2 all-reduce.3
  76.2 72.2 all-reduce.5
where the time goes:
time: 159 us
  waiting for transfers between devices  78.6 us (49%)
  blocking collectives  51.8 us (33%)
  between operations  17.5 us (11%)
  other arithmetic  7.02 us (4%)
  local copies, waits for them, and re-layouts  3.91 us (2%)
    psum x1, waiting for transfers between devices, full_sum(): return lax.psum(local_grad.astype(jnp.float32).astype(jnp.bfloat16), 'dp')  58 us
    psum x1, blocking collectives, local(): total_squares = lax.psum(squares, ('dp', 'fsdp'))  51.8 us
    psum x1, waiting for transfers between devices, from_root(): return lax.psum(jnp.where(mine, array, jnp.zeros_like(array)), axis)  19.9 us
  transfers between devices with their start and end apart: 2, of which 2 were waited for; matrix products, arithmetic and copies ran while one was open for 1% of the time, Pallas kernels for 0%

commit v1 on v0

v1 whole, which is shorter than its diff:
```python
import functools

import jax
import jax.numpy as jnp
from jax import lax
from jax.experimental import pallas as pl
from jax.experimental.pallas import tpu as pltpu
from jax.sharding import PartitionSpec as P

BETA = 0.95
EPSILON = 1e-06
MESH = pl.DeviceIdType.MESH
F32 = jnp.float32
BF16 = jnp.bfloat16


def mm(a, b):
    return jnp.dot(a, b, preferred_element_type=F32)


def mm_t(a, b):
    return lax.dot_general(a, b, (((1,), (1,)), ((), ())), preferred_element_type=F32)


class Stream:
    def __init__(self, me, order, block, source, kept, base, recv, part, whole, sems):
        self.order, self.block, self.n = order, block, len(order)
        self.source, self.kept, self.base = source, kept, base
        self.recv, self.part, self.whole = recv, part, whole
        self.rs_send, self.rs_recv, self.ag_send, self.ag_recv = sems
        self.bit = [(me // (1 << b)) % 2 for b in order]
        self.peer = [me + (1 - 2 * v) * (1 << b) for v, b in zip(self.bit, order)]
        self.half = [block >> (j + 1) for j in range(self.n)]
        self.at = [block - (block >> j) for j in range(self.n)]
        self.low = []
        low = 0
        for j in range(self.n):
            low = low + self.bit[j] * self.half[j]
            self.low.append(low)
        self.pending = []

    def rows(self, start, size):
        return pl.ds(pl.multiple_of(start, 16), size)

    def copy(self, src, dst, send, recv, peer):
        move = pltpu.make_async_remote_copy(
            src_ref=src,
            dst_ref=dst,
            send_sem=send,
            recv_sem=recv,
            device_id={"dp": peer},
            device_id_type=MESH,
        )
        move.start()
        self.pending.append(move)
        return move

    def start_sum(self, j):
        half = self.half[j]
        away = (1 - self.bit[j]) * half
        if j == 0:
            src = self.source.at[self.rows(self.base + away, half)]
        else:
            src = self.part.at[self.rows(self.at[j - 1] + away, half)]
        self.move = self.copy(
            src,
            self.recv.at[pl.ds(self.at[j], half)],
            self.rs_send.at[j],
            self.rs_recv.at[j],
            self.peer[j],
        )

    def added(self, j, offset, size):
        near = self.bit[j] * self.half[j] + offset
        if j == 0:
            mine = self.kept[self.rows(self.base + near, size), :]
        else:
            mine = self.part[self.rows(self.at[j - 1] + near, size), :]
        other = self.recv[self.rows(self.at[j] + offset, size), :]
        return (mine.astype(F32) + other.astype(F32)).astype(BF16)

    def end_sum(self, j):
        self.move.wait_recv()
        if j == self.n - 1:
            self.whole[self.rows(self.low[j], self.half[j]), :] = self.added(j, 0, self.half[j])
            self.start_spread(j)
            return
        quarter = self.half[j + 1]
        v = self.bit[j + 1]
        self.part[self.rows(self.at[j] + (1 - v) * quarter, quarter), :] = self.added(
            j, (1 - v) * quarter, quarter
        )
        self.start_sum(j + 1)
        self.part[self.rows(self.at[j] + v * quarter, quarter), :] = self.added(
            j, v * quarter, quarter
        )

    def start_spread(self, j):
        here = self.whole.at[self.rows(self.low[j], self.half[j])]
        self.move = self.copy(here, here, self.ag_send.at[j], self.ag_recv.at[j], self.peer[j])

    def end_spread(self, j):
        self.move.wait_recv()
        if j > 0:
            self.start_spread(j - 1)

    def finish(self):
        for move in self.pending:
            move.wait_send()


def kernel(
    n_dp, n_f, entries, owners, grads, stats, left, right, update, new_stats, new_root,
    v_grads, v_stats, v_left, v_right, masked, recv, part, whole, square_ref, rounded, outer_ref,
    slots, local_sem, rs_send, rs_recv, ag_send, ag_recv, z_send, z_recv,
):
    me = lax.axis_index("dp")
    col = lax.axis_index("fsdp")
    block = v_stats.shape[0]
    blocks = v_left.shape[0] // block
    bits = n_dp.bit_length() - 1

    loads = []
    for i, (src, dst) in enumerate(
        ((grads, v_grads), (stats, v_stats), (left, v_left), (right, v_right))
    ):
        load = pltpu.make_async_copy(src, dst, local_sem.at[i])
        load.start()
        loads.append(load)

    barrier = pltpu.get_barrier_semaphore()
    for b in range(bits):
        v = (me // (1 << b)) % 2
        pl.semaphore_signal(
            barrier, inc=1, device_id={"dp": me + (1 - 2 * v) * (1 << b)}, device_id_type=MESH
        )
    for o in range(1, n_f):
        pl.semaphore_signal(
            barrier, inc=1, device_id={"fsdp": lax.rem(col + o, n_f)}, device_id_type=MESH
        )
    pl.semaphore_wait(barrier, bits + n_f - 1)

    forward = list(range(bits))
    turned = [0] + forward[:0:-1]
    streams = []
    for k in range(2 * blocks):
        i = k % blocks
        of_grads = k < blocks
        streams.append(
            Stream(
                me, forward if i % 2 == 0 else turned, block,
                grads if of_grads else masked.at[i], v_grads if of_grads else masked.at[i],
                i * block if of_grads else 0,
                recv.at[k], part.at[k], whole.at[k],
                (rs_send.at[k], rs_recv.at[k], ag_send.at[k], ag_recv.at[k]),
            )
        )
    of_g, of_s = streams[:blocks], streams[blocks:]

    for s in of_g:
        s.start_sum(0)
    owns = [jnp.where(owners[col, i] == me, 1.0, 0.0).astype(F32) for i in range(blocks)]
    loads[1].wait()
    for i, s in enumerate(of_s):
        masked[i, :, :] = (v_stats[...] * owns[i]).astype(BF16)
        s.start_sum(0)
    loads[0].wait()
    for s in of_g:
        s.end_sum(0)
    for s in of_s:
        s.end_sum(0)
    loads[2].wait()
    for i in range(blocks):
        x = v_left[pl.ds(i * block, block), :]
        square_ref[i, :, :] = mm(x, x).astype(BF16)
    for j in range(1, bits):
        for s in streams:
            s.end_sum(j)
    for j in range(bits - 1, 0, -1):
        for s in of_g:
            s.end_spread(j)
        if j > 1:
            for s in of_s:
                s.end_spread(j)
    loads[3].wait()
    squares = jnp.zeros((8, 128), F32)
    for i, s in enumerate(of_g):
        s.end_spread(0)
        rows = pl.ds(i * block, block)
        product = mm(v_left[rows, :], whole[i, :, :]).astype(BF16)
        raw = mm(product, v_right[rows, :])
        rounded[rows, :] = raw.astype(BF16)
        power = jnp.sum((raw * raw).reshape(block // 8, 8, block), axis=0)
        for c in range(0, block, 128):
            squares = squares + power[:, c : c + 128]
    slots[pl.ds(col, 1), :, :] = squares[None]
    z_moves = []
    for o in range(1, n_f):
        move = pltpu.make_async_remote_copy(
            src_ref=slots.at[col],
            dst_ref=slots.at[col],
            send_sem=z_send.at[o - 1],
            recv_sem=z_recv.at[o - 1],
            device_id={"fsdp": lax.rem(col + o, n_f)},
            device_id_type=MESH,
        )
        move.start()
        z_moves.append(move)
    if bits > 1:
        for s in of_s:
            s.end_spread(1)
    for i in range(blocks):
        g = whole[i, :, :]
        outer_ref[i, :, :] = (1.0 - BETA) * mm_t(g, g)
    mine = BETA * v_stats[...] * sum(owns[1:], owns[0])
    for i in range(blocks):
        mine = mine + owns[i] * outer_ref[i, :, :]
    new_stats[...] = mine
    for i, s in enumerate(of_s):
        s.end_spread(0)
        x = v_left[pl.ds(i * block, block), :]
        q = square_ref[i, :, :]
        fresh = BETA * whole[blocks + i, :, :].astype(F32) + outer_ref[i, :, :]
        half_way = mm(q, fresh.astype(BF16)).astype(BF16)
        middle = mm(half_way, q).astype(BF16)
        new_root[pl.ds(i * block, block), :] = (
            1.25 * x.astype(F32) - 0.25 * mm(x, middle)
        ).astype(BF16)
    for move in z_moves:
        move.wait_recv()
    total = slots[0]
    for c in range(1, n_f):
        total = total + slots[c]
    total = jnp.sum(jnp.sum(total, axis=1, keepdims=True), axis=0, keepdims=True)
    scale = lax.rsqrt(total / entries + EPSILON)
    update[...] = (rounded[...].astype(F32) * scale).astype(BF16)
    for s in streams:
        s.finish()
    for move in z_moves:
        move.wait_send()


def solution(mesh):
    n_dp, n_f = mesh.shape["dp"], mesh.shape["fsdp"]
    bits = n_dp.bit_length() - 1

    def local(grads, stats, left, right, owners):
        block = stats.shape[-1]
        rows = left.shape[0]
        blocks = rows // block
        hbm = pl.BlockSpec(memory_space=pl.ANY)
        vmem = pl.BlockSpec(memory_space=pltpu.VMEM)
        dma = pltpu.SemaphoreType.DMA
        update, new_stats, new_root = pl.pallas_call(
            functools.partial(kernel, n_dp, n_f, rows * block * n_f),
            out_shape=(
                jax.ShapeDtypeStruct((rows, block), BF16),
                jax.ShapeDtypeStruct((block, block), F32),
                jax.ShapeDtypeStruct((rows, block), BF16),
            ),
            in_specs=[pl.BlockSpec(memory_space=pltpu.SMEM), hbm, hbm, hbm, hbm],
            out_specs=(vmem, vmem, vmem),
            scratch_shapes=[
                pltpu.VMEM((rows, block), BF16),
                pltpu.VMEM((block, block), F32),
                pltpu.VMEM((rows, block), BF16),
                pltpu.VMEM((rows, block), BF16),
                pltpu.VMEM((blocks, block, block), BF16),
                pltpu.VMEM((2 * blocks, block, block), BF16),
                pltpu.VMEM((2 * blocks, block, block), BF16),
                pltpu.VMEM((2 * blocks, block, block), BF16),
                pltpu.VMEM((blocks, block, block), BF16),
                pltpu.VMEM((rows, block), BF16),
                pltpu.VMEM((blocks, block, block), F32),
                pltpu.VMEM((n_f, 8, 128), F32),
                dma((4,)),
                dma((2 * blocks, bits)),
                dma((2 * blocks, bits)),
                dma((2 * blocks, bits)),
                dma((2 * blocks, bits)),
                dma((max(n_f - 1, 1),)),
                dma((max(n_f - 1, 1),)),
            ],
            compiler_params=pltpu.CompilerParams(
                collective_id=0, has_side_effects=True, vmem_limit_bytes=48 << 20
            ),
        )(owners, grads[0], stats[0, 0], left, right)
        return update, new_stats[None, None], new_root

    in_specs = (
        P("dp", None, "fsdp"),
        P("dp", "fsdp", None, None),
        P(None, "fsdp"),
        P(None, "fsdp"),
        P(),
    )
    out_specs = (P(None, "fsdp"), P("dp", "fsdp", None, None), P(None, "fsdp"))
    return jax.shard_map(local, mesh=mesh, in_specs=in_specs, out_specs=out_specs, check_vma=False)
```

time: 159 us -> 40.1 us (0.25)
  waiting for transfers between devices: 78.6 us -> 0 us
  blocking collectives: 51.8 us -> 0 us
  Pallas kernels: 0 us -> 33.1 us
  between operations: 17.5 us -> 0.65 us
  other arithmetic: 7.02 us -> 0 us
  local copies, waits for them, and re-layouts: 3.91 us -> 6.12 us
    psum x2 -> x0, waiting for transfers between devices: 77.9 us -> none  [the longest x1 58 us: full_sum(): return lax.psum(local_grad.astype(jnp.float32).astype(jnp.bfloat16), 'dp')]
    psum x1 -> x0, blocking collectives: 51.8 us -> none  [local(): total_squares = lax.psum(squares, ('dp', 'fsdp'))]
    pallas_call x0 -> x1, Pallas kernels: none -> 33.1 us  [local(): pl.pallas_call(functools.partial(kernel, n_dp, n_f, rows * block * n_f),...]
    unnamed x12 -> x10, local copies, waits for them, and re-layouts: 0.99 us -> 6.12 us
    concatenate x2 -> x0, other arithmetic: 3.36 us -> none  [the longest x1 2.33 us: local(): new_root = jnp.concatenate(root_pieces, axis=0)]
    select_n x2 -> x0, other arithmetic: 2.1 us -> none  [from_root(): return lax.psum(jnp.where(mine, array, jnp.zeros_like(array)), axis)]
  transfers between devices with their start and end apart: 2 -> 0, of which waited for: 2 -> 0; matrix products, arithmetic and copies ran while one was open for 1% -> 0% of each run, Pallas kernels for 0% -> 0%
where the time goes in v1:
time: 40.1 us; the launch traced here: 39.9 us
  Pallas kernels  33.1 us (83%)
  local copies, waits for them, and re-layouts  6.12 us (15%)
  between operations  0.65 us (2%)
    pallas_call x1, Pallas kernels, local(): pl.pallas_call(functools.partial(kernel, n_dp, n_f, rows * block * n_f),...  33.1 us
    unnamed x10, local copies, waits for them, and re-layouts  6.12 us

profile of v1, /device:TPU:0, one launch (start us, length us, event | category | flops | bytes accessed | tf_op | source)
XLA Modules:
  0.0 39.9 jit_solution(3099489983482635769)
XLA Ops:
  0.6 0.0 copy-start.2
  0.6 0.7 %copy-done.2 = s32[4,2]{0,1:T(2,128)S(1)} copy-done((s32[4,2]{0,1:T(2,128)S(1)}, s32[4,2]{0,1:T(2,128)}, u32[]{:S(2)}) %copy-start.2) | copy-done | bytes 56
  1.3 0.1 copy.8.owners
  1.4 0.0 copy-start
  1.4 1.2 %copy-done = bf16[1,1024,512]{2,1,0:T(8,128)(2,1)S(1)} copy-done((bf16[1,1024,512]{2,1,0:T(8,128)(2,1)S(1)}, bf16[1,1024,512]{2,1,0:T(8,128)(2,1)}, u32[]{:S(2)}) %copy-start) | copy-done | bytes 1048600
  2.6 0.0 copy-start.1
  2.6 1.2 %copy-done.1 = f32[1,1,512,512]{3,2,1,0:T(8,128)S(1)} copy-done((f32[1,1,512,512]{3,2,1,0:T(8,128)S(1)}, f32[1,1,512,512]{3,2,1,0:T(8,128)}, u32[]{:S(2)}) %copy-start.1) | copy-done | bytes 1048600
  3.9 33.1 %shard_map.76 = (bf16[1024,512]{1,0:T(8,128)(2,1)S(1)}, f32[512,512]{1,0:T(8,128)S(1)}, bf16[1024,512]{1,0:T(8,128)(2,1)S(1)}) custom-call(s32[4,2]{1,0:T(4,128)S(1)} %copy.8.owners, bf16[1024,512]{1,0:T(8,128)(2,1)S(1)} %bitcast.4, f32[512,512]{1,0:T(8,128)S(1)} %bitcast.5, bf16[1024,512]{1,0:T(8,128)(2,1)} %left.1, bf16[1024,512]{1,0:T(8,128)(2,1)} %right.1), custom_call_target="tpu_custom_call" | custom-call | tf_op jit(solution)/shard_map/pallas_call | solution.py:254
  37.0 1.0 %copy.12 = bf16[1024,512]{1,0:T(8,128)(2,1)} copy(bf16[1024,512]{1,0:T(8,128)(2,1)S(1)} %get-tuple-element.12) | data formatting | bytes 2097152
  38.0 1.0 %copy.13 = f32[1,1,512,512]{3,2,1,0:T(8,128)} copy(f32[1,1,512,512]{3,2,1,0:T(8,128)S(1)} %bitcast.3) | data formatting | bytes 2097152
  38.9 1.0 %copy.14 = bf16[1024,512]{1,0:T(8,128)(2,1)} copy(bf16[1024,512]{1,0:T(8,128)(2,1)S(1)} %get-tuple-element.14) | data formatting | bytes 2097152
Async XLA Ops:
  0.6 0.7 %copy-start.2 = (s32[4,2]{0,1:T(2,128)S(1)}, s32[4,2]{0,1:T(2,128)}, u32[]{:S(2)}) copy-start(s32[4,2]{0,1:T(2,128)} %param.9) | copy-start | bytes 100
  1.4 1.2 %copy-start = (bf16[1,1024,512]{2,1,0:T(8,128)(2,1)S(1)}, bf16[1,1024,512]{2,1,0:T(8,128)(2,1)}, u32[]{:S(2)}) copy-start(bf16[1,1024,512]{2,1,0:T(8,128)(2,1)} %param.5) | copy-start | bytes 3145732
  2.6 1.2 %copy-start.1 = (f32[1,1,512,512]{3,2,1,0:T(8,128)S(1)}, f32[1,1,512,512]{3,2,1,0:T(8,128)}, u32[]{:S(2)}) copy-start(f32[1,1,512,512]{3,2,1,0:T(8,128)} %param.6) | copy-start | bytes 3145732

commit v2 on v1

--- a/solution.py
+++ b/solution.py
@@ -109,9 +109,15 @@
             move.wait_send()
 
 
+def tile_list(count, upper):
+    return [(r, c) for r in range(count) for c in range(r if upper else 0, count)]
+
+
 def kernel(
-    n_dp, n_f, entries, owners, grads, stats, left, right, update, new_stats, new_root,
-    v_grads, v_stats, v_left, v_right, masked, recv, part, whole, square_ref, rounded, outer_ref,
+    n_dp, n_f, entries, tiles, upper, owners_hbm, grads, stats, left, right,
+    update, new_stats, new_root,
+    owners, v_grads, v_stats, v_left, v_right, masked, recv_g, part_g, whole_g,
+    recv_a, part_a, whole_a, full, square_ref, rounded, base_ref,
     slots, local_sem, rs_send, rs_recv, ag_send, ag_recv, z_send, z_recv,
 ):
     me = lax.axis_index("dp")
@@ -122,7 +128,10 @@
 
     loads = []
     for i, (src, dst) in enumerate(
-        ((grads, v_grads), (stats, v_stats), (left, v_left), (right, v_right))
+        (
+            (owners_hbm, owners), (stats.at[0, 0], v_stats), (left, v_left),
+            (grads.at[0], v_grads), (right, v_right),
+        )
     ):
         load = pltpu.make_async_copy(src, dst, local_sem.at[i])
         load.start()
@@ -142,34 +151,47 @@
 
     forward = list(range(bits))
     turned = [0] + forward[:0:-1]
-    streams = []
-    for k in range(2 * blocks):
-        i = k % blocks
-        of_grads = k < blocks
-        streams.append(
+    of_g, of_a = [], []
+    for i in range(blocks):
+        order = forward if i % 2 == 0 else turned
+        k = blocks + i
+        of_g.append(
             Stream(
-                me, forward if i % 2 == 0 else turned, block,
-                grads if of_grads else masked.at[i], v_grads if of_grads else masked.at[i],
-                i * block if of_grads else 0,
-                recv.at[k], part.at[k], whole.at[k],
+                me, order, block, grads.at[0], v_grads, i * block,
+                recv_g.at[i], part_g.at[i], whole_g.at[i],
+                (rs_send.at[i], rs_recv.at[i], ag_send.at[i], ag_recv.at[i]),
+            )
+        )
+        of_a.append(
+            Stream(
+                me, order, masked.shape[1], masked.at[i], masked.at[i], 0,
+                recv_a.at[i], part_a.at[i], whole_a.at[i],
                 (rs_send.at[k], rs_recv.at[k], ag_send.at[k], ag_recv.at[k]),
             )
         )
-    of_g, of_s = streams[:blocks], streams[blocks:]
+    streams = of_g + of_a
 
     for s in of_g:
         s.start_sum(0)
-    owns = [jnp.where(owners[col, i] == me, 1.0, 0.0).astype(F32) for i in range(blocks)]
-    loads[1].wait()
-    for i, s in enumerate(of_s):
-        masked[i, :, :] = (v_stats[...] * owns[i]).astype(BF16)
+    for load in loads[:3]:
+        load.wait()
+    owns = [jnp.where(owners[i, col] == me, 1.0, 0.0).astype(F32) for i in range(blocks)]
+    own_x = jnp.zeros((block, block), F32)
+    for i in range(blocks):
+        own_x = own_x + owns[i] * v_left[pl.ds(i * block, block), :].astype(F32)
+    own_x = own_x.astype(BF16)
+    own_q = mm(own_x, own_x).astype(BF16)
+    own_a = mm(mm(own_q, v_stats[...].astype(BF16)).astype(BF16), own_q)
+    for i, s in enumerate(of_a):
+        mine = (own_a * owns[i]).astype(BF16)
+        for k, (r, c) in enumerate(tiles):
+            masked[i, pl.ds(k * 128, 128), :] = mine[
+                r * 128 : (r + 1) * 128, c * 128 : (c + 1) * 128
+            ]
         s.start_sum(0)
-    loads[0].wait()
-    for s in of_g:
+    loads[3].wait()
+    for s in streams:
         s.end_sum(0)
-    for s in of_s:
-        s.end_sum(0)
-    loads[2].wait()
     for i in range(blocks):
         x = v_left[pl.ds(i * block, block), :]
         square_ref[i, :, :] = mm(x, x).astype(BF16)
@@ -180,14 +202,14 @@
         for s in of_g:
             s.end_spread(j)
         if j > 1:
-            for s in of_s:
+            for s in of_a:
                 s.end_spread(j)
-    loads[3].wait()
+    loads[4].wait()
     squares = jnp.zeros((8, 128), F32)
     for i, s in enumerate(of_g):
         s.end_spread(0)
         rows = pl.ds(i * block, block)
-        product = mm(v_left[rows, :], whole[i, :, :]).astype(BF16)
+        product = mm(v_left[rows, :], whole_g[i, :, :]).astype(BF16)
         raw = mm(product, v_right[rows, :])
         rounded[rows, :] = raw.astype(BF16)
         power = jnp.sum((raw * raw).reshape(block // 8, 8, block), axis=0)
@@ -207,25 +229,17 @@
         move.start()
         z_moves.append(move)
     if bits > 1:
-        for s in of_s:
+        for s in of_a:
             s.end_spread(1)
+    outer = jnp.zeros((block, block), F32)
     for i in range(blocks):
-        g = whole[i, :, :]
-        outer_ref[i, :, :] = (1.0 - BETA) * mm_t(g, g)
-    mine = BETA * v_stats[...] * sum(owns[1:], owns[0])
-    for i in range(blocks):
-        mine = mine + owns[i] * outer_ref[i, :, :]
-    new_stats[...] = mine
-    for i, s in enumerate(of_s):
-        s.end_spread(0)
+        g = whole_g[i, :, :]
         x = v_left[pl.ds(i * block, block), :]
-        q = square_ref[i, :, :]
-        fresh = BETA * whole[blocks + i, :, :].astype(F32) + outer_ref[i, :, :]
-        half_way = mm(q, fresh.astype(BF16)).astype(BF16)
-        middle = mm(half_way, q).astype(BF16)
-        new_root[pl.ds(i * block, block), :] = (
-            1.25 * x.astype(F32) - 0.25 * mm(x, middle)
-        ).astype(BF16)
+        h = mm(square_ref[i, :, :], g).astype(BF16)
+        extra = (((1.0 - BETA) * 0.25) * mm_t(h, h)).astype(BF16)
+        base_ref[i, :, :] = 1.25 * x.astype(F32) - mm(x, extra)
+        outer = outer + (owns[i] * (1.0 - BETA)) * mm_t(g, g)
+    new_stats[...] = (BETA * sum(owns[1:], owns[0])) * v_stats[...] + outer
     for move in z_moves:
         move.wait_recv()
     total = slots[0]
@@ -234,12 +248,35 @@
     total = jnp.sum(jnp.sum(total, axis=1, keepdims=True), axis=0, keepdims=True)
     scale = lax.rsqrt(total / entries + EPSILON)
     update[...] = (rounded[...].astype(F32) * scale).astype(BF16)
+    for i, s in enumerate(of_a):
+        s.end_spread(0)
+        for k, (r, c) in enumerate(tiles):
+            tile = whole_a[i, pl.ds(k * 128, 128), :]
+            full[i, pl.ds(r * 128, 128), pl.ds(c * 128, 128)] = tile
+            if upper and r != c:
+                full[i, pl.ds(c * 128, 128), pl.ds(r * 128, 128)] = tile.T
+        rows = pl.ds(i * block, block)
+        new_root[rows, :] = (
+            base_ref[i, :, :] - (BETA * 0.25) * mm(v_left[rows, :], full[i, :, :])
+        ).astype(BF16)
     for s in streams:
         s.finish()
     for move in z_moves:
         move.wait_send()
 
 
+def write_out(*refs):
+    sources, targets, sems = refs[:3], refs[3:6], refs[6]
+    moves = [
+        pltpu.make_async_copy(src, dst, sems.at[i])
+        for i, (src, dst) in enumerate(zip(sources, targets))
+    ]
+    for move in moves:
+        move.start()
+    for move in moves:
+        move.wait()
+
+
 def solution(mesh):
     n_dp, n_f = mesh.shape["dp"], mesh.shape["fsdp"]
     bits = n_dp.bit_length() - 1
@@ -248,32 +285,42 @@
         block = stats.shape[-1]
         rows = left.shape[0]
         blocks = rows // block
+        count = block // 128
+        upper = (len(tile_list(count, True)) * 128) % (16 * n_dp) == 0
+        tiles = tile_list(count, upper)
+        size = len(tiles) * 128
         hbm = pl.BlockSpec(memory_space=pl.ANY)
         vmem = pl.BlockSpec(memory_space=pltpu.VMEM)
         dma = pltpu.SemaphoreType.DMA
-        update, new_stats, new_root = pl.pallas_call(
-            functools.partial(kernel, n_dp, n_f, rows * block * n_f),
-            out_shape=(
-                jax.ShapeDtypeStruct((rows, block), BF16),
-                jax.ShapeDtypeStruct((block, block), F32),
-                jax.ShapeDtypeStruct((rows, block), BF16),
-            ),
-            in_specs=[pl.BlockSpec(memory_space=pltpu.SMEM), hbm, hbm, hbm, hbm],
+        shapes = (
+            jax.ShapeDtypeStruct((rows, block), BF16),
+            jax.ShapeDtypeStruct((block, block), F32),
+            jax.ShapeDtypeStruct((rows, block), BF16),
+        )
+        results = pl.pallas_call(
+            functools.partial(kernel, n_dp, n_f, rows * block * n_f, tiles, upper),
+            out_shape=shapes,
+            in_specs=[pl.BlockSpec(memory_space=pltpu.HBM)] * 5,
             out_specs=(vmem, vmem, vmem),
             scratch_shapes=[
+                pltpu.SMEM((blocks, n_f), jnp.int32),
                 pltpu.VMEM((rows, block), BF16),
                 pltpu.VMEM((block, block), F32),
                 pltpu.VMEM((rows, block), BF16),
                 pltpu.VMEM((rows, block), BF16),
-                pltpu.VMEM((blocks, block, block), BF16),
-                pltpu.VMEM((2 * blocks, block, block), BF16),
-                pltpu.VMEM((2 * blocks, block, block), BF16),
-                pltpu.VMEM((2 * blocks, block, block), BF16),
+                pltpu.VMEM((blocks, size, 128), BF16),
+                pltpu.VMEM((blocks, block, block), BF16),
+                pltpu.VMEM((blocks, block, block), BF16),
+                pltpu.VMEM((blocks, block, block), BF16),
+                pltpu.VMEM((blocks, size, 128), BF16),
+                pltpu.VMEM((blocks, size, 128), BF16),
+                pltpu.VMEM((blocks, size, 128), BF16),
+                pltpu.VMEM((blocks, block, block), BF16),
                 pltpu.VMEM((blocks, block, block), BF16),
                 pltpu.VMEM((rows, block), BF16),
                 pltpu.VMEM((blocks, block, block), F32),
                 pltpu.VMEM((n_f, 8, 128), F32),
-                dma((4,)),
+                dma((5,)),
                 dma((2 * blocks, bits)),
                 dma((2 * blocks, bits)),
                 dma((2 * blocks, bits)),
@@ -282,9 +329,17 @@
                 dma((max(n_f - 1, 1),)),
             ],
             compiler_params=pltpu.CompilerParams(
-                collective_id=0, has_side_effects=True, vmem_limit_bytes=48 << 20
+                collective_id=0, has_side_effects=True, vmem_limit_bytes=50 << 20
             ),
-        )(owners, grads[0], stats[0, 0], left, right)
+        )(owners.T, grads, stats, left, right)
+        update, new_stats, new_root = pl.pallas_call(
+            write_out,
+            out_shape=shapes,
+            in_specs=[hbm] * 3,
+            out_specs=(hbm, hbm, hbm),
+            scratch_shapes=[dma((3,))],
+            compiler_params=pltpu.CompilerParams(vmem_limit_bytes=50 << 20),
+        )(*results)
         return update, new_stats[None, None], new_root
 
     in_specs = (

time: 40.1 us -> 33.9 us (0.85)
  local copies, waits for them, and re-layouts: 6.12 us -> 0.67 us
  Pallas kernels: 33.1 us -> 32.4 us
    unnamed x10 -> x2, local copies, waits for them, and re-layouts: 6.12 us -> 0.67 us
    pallas_call x1 -> x2, Pallas kernels: 33.1 us -> 32.4 us  [the longest x1 30.7 us: local(): pl.pallas_call(functools.partial(kernel, n_dp, n_f, rows * block * n_f, t...]
where the time goes in v2:
time: 33.9 us; the launch traced here: 33.7 us
  Pallas kernels  32.4 us (96%)
  local copies, waits for them, and re-layouts  0.67 us (2%)
  between operations  0.65 us (2%)
    pallas_call x1, Pallas kernels, local(): pl.pallas_call(functools.partial(kernel, n_dp, n_f, rows * block * n_f, t...  30.7 us
    pallas_call x1, Pallas kernels, local(): pl.pallas_call(write_out, out_shape=shapes, in_specs=[hbm] * 3, out_specs...  1.69 us

profile of v2, /device:TPU:0, one launch (start us, length us, event | category | flops | bytes accessed | tf_op | source)
XLA Modules:
  0.0 33.7 jit_solution(17930341582740814979)
XLA Ops:
  0.6 0.0 copy-start
  0.6 0.7 %copy-done = s32[4,2]{0,1:T(2,128)S(1)} copy-done((s32[4,2]{0,1:T(2,128)S(1)}, s32[4,2]{0,1:T(2,128)}, u32[]{:S(2)}) %copy-start) | copy-done | bytes 56
  1.3 30.7 %shard_map.76 = (bf16[1024,512]{1,0:T(8,128)(2,1)S(1)}, f32[512,512]{1,0:T(8,128)S(1)}, bf16[1024,512]{1,0:T(8,128)(2,1)S(1)}) custom-call(s32[2,4]{1,0:T(2,128)S(1)} %bitcast.2, bf16[1,1024,512]{2,1,0:T(8,128)(2,1)} %grads.1, f32[1,1,512,512]{3,2,1,0:T(8,128)} %stats.1, bf16[1024,512]{1,0:T(8,128)(2,1)} %left.1, bf16[1024,512]{1,0:T(8,128)(2,1)} %right.1), custom_call_target="tpu_custom_call" | custom-call | tf_op jit(solution)/shard_map/pallas_call | solution.py:300
  32.0 1.7 %shard_map.77 = (bf16[1024,512]{1,0:T(8,128)(2,1)}, f32[512,512]{1,0:T(8,128)}, bf16[1024,512]{1,0:T(8,128)(2,1)}) custom-call(bf16[1024,512]{1,0:T(8,128)(2,1)S(1)} %get-tuple-element.9.refs_0_, f32[512,512]{1,0:T(8,128)S(1)} %get-tuple-element.10.refs_1_, bf16[1024,512]{1,0:T(8,128)(2,1)S(1)} %get-tuple-element.11.refs_2_), custom_call_target="tpu_custom_call" | custom-call | tf_op jit(solution)/shard_map/pallas_call | solution.py:335
Async XLA Ops:
  0.6 0.7 %copy-start = (s32[4,2]{0,1:T(2,128)S(1)}, s32[4,2]{0,1:T(2,128)}, u32[]{:S(2)}) copy-start(s32[4,2]{0,1:T(2,128)} %param.9) | copy-start | bytes 100

commit v3 on v2

v3 whole, which is shorter than its diff:
```python
import functools

import jax
import jax.numpy as jnp
from jax import lax
from jax.experimental import pallas as pl
from jax.experimental.pallas import tpu as pltpu
from jax.sharding import PartitionSpec as P

BETA = 0.95
EPSILON = 1e-06
MESH = pl.DeviceIdType.MESH
F32 = jnp.float32
BF16 = jnp.bfloat16


def mm(a, b):
    return jnp.dot(a, b, preferred_element_type=F32)


def mm_t(a, b):
    return lax.dot_general(a, b, (((1,), (1,)), ((), ())), preferred_element_type=F32)


class Stream:
    def __init__(self, me, order, size, source, kept, near, away, recv, part, whole, base, sems):
        self.order, self.size, self.n = order, size, len(order)
        self.source, self.kept, self.near, self.away = source, kept, near, away
        self.recv, self.part, self.whole = recv, part, whole
        self.rs_send, self.rs_recv, self.ag_send, self.ag_recv = sems
        self.bit = [(me // (1 << b)) % 2 for b in order]
        self.peer = [me + (1 - 2 * v) * (1 << b) for v, b in zip(self.bit, order)]
        self.half = [size >> j for j in range(self.n)]
        self.at = [0] + [2 * size - (size >> (j - 1)) for j in range(1, self.n)]
        self.low = [base]
        for j in range(1, self.n):
            self.low.append(self.low[-1] + self.bit[j] * self.half[j])
        self.pending = []

    def rows(self, start, size):
        return pl.ds(pl.multiple_of(start, 16), size)

    def copy(self, src, dst, send, recv, peer):
        move = pltpu.make_async_remote_copy(
            src_ref=src,
            dst_ref=dst,
            send_sem=send,
            recv_sem=recv,
            device_id={"dp": peer},
            device_id_type=MESH,
        )
        move.start()
        self.pending.append(move)
        return move

    def start_sum(self, j):
        half = self.half[j]
        if j == 0:
            src = self.source.at[self.rows(self.away, half)]
        else:
            src = self.part.at[self.rows(self.at[j - 1] + (1 - self.bit[j]) * half, half)]
        self.move = self.copy(
            src,
            self.recv.at[pl.ds(self.at[j], half)],
            self.rs_send.at[j],
            self.rs_recv.at[j],
            self.peer[j],
        )

    def added(self, j, offset, size):
        if j == 0:
            mine = self.kept[self.rows(self.near + offset, size), :]
        else:
            near = self.at[j - 1] + self.bit[j] * self.half[j]
            mine = self.part[self.rows(near + offset, size), :]
        other = self.recv[self.rows(self.at[j] + offset, size), :]
        return (mine.astype(F32) + other.astype(F32)).astype(BF16)

    def end_sum(self, j):
        self.move.wait_recv()
        if j == self.n - 1:
            self.whole[self.rows(self.low[j], self.half[j]), :] = self.added(j, 0, self.half[j])
            if j > 0:
                self.start_spread(j)
            return
        quarter = self.half[j + 1]
        v = self.bit[j + 1]
        self.part[self.rows(self.at[j] + (1 - v) * quarter, quarter), :] = self.added(
            j, (1 - v) * quarter, quarter
        )
        self.start_sum(j + 1)
        self.part[self.rows(self.at[j] + v * quarter, quarter), :] = self.added(
            j, v * quarter, quarter
        )

    def start_spread(self, j):
        here = self.whole.at[self.rows(self.low[j], self.half[j])]
        self.move = self.copy(here, here, self.ag_send.at[j], self.ag_recv.at[j], self.peer[j])

    def end_spread(self, j):
        self.move.wait_recv()
        if j > 1:
            self.start_spread(j - 1)

    def finish(self):
        for move in self.pending:
            move.wait_send()


def tile_list(count, upper):
    return [(r, c) for r in range(count) for c in range(r if upper else 0, count)]


def kernel(
    n_dp, n_f, entries, tiles, upper, owners_hbm, grads, stats, left, right,
    update, new_stats, new_root,
    owners, v_grads, v_stats, v_left, v_right, masked, recv_g, part_g, whole_g,
    recv_a, part_a, whole_a, full, rounded, extra,
    slots, local_sem, rs_send, rs_recv, ag_send, ag_recv, x_send, x_recv, z_send, z_recv,
):
    me = lax.axis_index("dp")
    col = lax.axis_index("fsdp")
    block = v_stats.shape[0]
    size = whole_a.shape[0]
    bits = n_dp.bit_length() - 1
    core = me % 2
    twin = me + 1 - 2 * core
    here = pl.ds(pl.multiple_of(core * block, block), block)

    loads = []
    for i, (src, dst) in enumerate(
        (
            (owners_hbm, owners), (stats.at[0, 0], v_stats), (left, v_left),
            (grads.at[0], v_grads), (right.at[here], v_right),
        )
    ):
        load = pltpu.make_async_copy(src, dst, local_sem.at[i])
        load.start()
        loads.append(load)

    partners = [{"dp": me + (1 - 2 * ((me // (1 << b)) % 2)) * (1 << b)} for b in range(bits)]
    others = []
    for o in range(1, n_f):
        others.append({"fsdp": lax.rem(col + o, n_f)})
        others.append({"dp": twin, "fsdp": lax.rem(col + o, n_f)})
    barrier = pltpu.get_barrier_semaphore()
    for device in partners + others:
        pl.semaphore_signal(barrier, inc=1, device_id=device, device_id_type=MESH)
    pl.semaphore_wait(barrier, len(partners) + len(others))
    others.append({"dp": twin})

    forward = list(range(bits))
    turned = [0] + forward[:0:-1]
    of_g, of_a = [], []
    for k in range(2):
        order = forward if k == 0 else turned
        share = block // 2
        of_g.append(
            Stream(
                me, order, share, grads.at[0], v_grads,
                core * block + k * share, (1 - core) * block + k * share,
                recv_g.at[k], part_g.at[k], whole_g, core * block + k * share,
                (rs_send.at[k], rs_recv.at[k], ag_send.at[k], ag_recv.at[k]),
            )
        )
        share = size // 2
        of_a.append(
            Stream(
                me, order, share, masked, masked,
                core * size + k * share, (1 - core) * size + k * share,
                recv_a.at[k], part_a.at[k], whole_a, k * share,
                (rs_send.at[2 + k], rs_recv.at[2 + k], ag_send.at[2 + k], ag_recv.at[2 + k]),
            )
        )
    streams = of_g + of_a
    swaps = []

    def swap(src, dst):
        move = pltpu.make_async_remote_copy(
            src_ref=src,
            dst_ref=dst,
            send_sem=x_send.at[len(swaps)],
            recv_sem=x_recv.at[len(swaps)],
            device_id={"dp": twin},
            device_id_type=MESH,
        )
        move.start()
        swaps.append(move)

    for s in of_g:
        s.start_sum(0)
    for load in loads[:3]:
        load.wait()
    owns = [jnp.where(owners[i, col] == me, 1.0, 0.0).astype(F32) for i in range(2)]

    def owned(ref):
        first = owns[0] * ref[pl.ds(0, block), :].astype(F32)
        return (first + owns[1] * ref[pl.ds(block, block), :].astype(F32)).astype(BF16)

    own_x = owned(v_left)
    own_q = mm(own_x, own_x).astype(BF16)
    own_t = mm(own_q, v_stats[...].astype(BF16)).astype(BF16)
    loads[3].wait()
    for s in of_g:
        s.end_sum(0)
    own_a = mm(own_t, own_q)
    for i in range(2):
        mine = (own_a * owns[i]).astype(BF16)
        for k, (r, c) in enumerate(tiles):
            masked[pl.ds(i * size + k * 128, 128), :] = mine[
                r * 128 : (r + 1) * 128, c * 128 : (c + 1) * 128
            ]
    for s in of_a:
        s.start_sum(0)
    x = v_left[here, :]
    q = mm(x, x).astype(BF16)
    for s in of_a:
        s.end_sum(0)
    for j in range(1, bits):
        for s in streams:
            s.end_sum(j)
    for j in range(bits - 1, 0, -1):
        for s in of_g:
            s.end_spread(j)
        if j > 1:
            for s in of_a:
                s.end_spread(j)
    swap(whole_g.at[here], whole_g.at[here])
    loads[4].wait()
    g = whole_g[here, :]
    raw = mm(mm(x, g).astype(BF16), v_right[...])
    rounded[here, :] = raw.astype(BF16)
    swap(rounded.at[here], rounded.at[here])
    power = jnp.sum((raw * raw).reshape(block // 8, 8, block), axis=0)
    squares = jnp.zeros((8, 128), F32)
    for c in range(0, block, 128):
        squares = squares + power[:, c : c + 128]
    slot = core * n_f + col
    slots[pl.ds(slot, 1), :, :] = squares[None]
    z_moves = []
    for i, device in enumerate(others):
        move = pltpu.make_async_remote_copy(
            src_ref=slots.at[slot],
            dst_ref=slots.at[slot],
            send_sem=z_send.at[i],
            recv_sem=z_recv.at[i],
            device_id=device,
            device_id_type=MESH,
        )
        move.start()
        z_moves.append(move)
    h = mm(q, g).astype(BF16)
    extra[...] = (1.0 - BETA) * mm_t(h, h)
    swaps[0].wait_recv()
    own_g = owned(whole_g)
    has = owns[0] + owns[1]
    new_stats[...] = (BETA * has) * v_stats[...] + (1.0 - BETA) * mm_t(own_g, own_g)
    for move in z_moves:
        move.wait_recv()
    total = slots[0]
    for c in range(1, 2 * n_f):
        total = total + slots[c]
    total = jnp.sum(jnp.sum(total, axis=1, keepdims=True), axis=0, keepdims=True)
    scale = lax.rsqrt(total / entries + EPSILON)
    swaps[1].wait_recv()
    update[...] = (rounded[...].astype(F32) * scale).astype(BF16)
    if bits > 1:
        for s in of_a:
            s.end_spread(1)
    for k, (r, c) in enumerate(tiles):
        down, along = pl.ds(r * 128, 128), pl.ds(c * 128, 128)
        middle = BETA * whole_a[pl.ds(k * 128, 128), :].astype(F32) + extra[down, along]
        middle = middle.astype(BF16)
        full[down, along] = middle
        if upper and r != c:
            full[along, down] = middle.T
    middle = full[...]
    share = block // 2
    for k in range(2):
        rows = pl.ds(pl.multiple_of(core * block + k * share, share), share)
        some = v_left[rows, :]
        new_root[rows, :] = (1.25 * some.astype(F32) - 0.25 * mm(some, middle)).astype(BF16)
        swap(new_root.at[rows], new_root.at[rows])
    for move in swaps[2:]:
        move.wait_recv()
    for s in streams:
        s.finish()
    for move in swaps + z_moves:
        move.wait_send()


def write_out(*refs):
    sources, targets, sems = refs[:3], refs[3:6], refs[6]
    moves = [
        pltpu.make_async_copy(src, dst, sems.at[i])
        for i, (src, dst) in enumerate(zip(sources, targets))
    ]
    for move in moves:
        move.start()
    for move in moves:
        move.wait()


def solution(mesh):
    n_dp, n_f = mesh.shape["dp"], mesh.shape["fsdp"]
    bits = n_dp.bit_length() - 1

    def local(grads, stats, left, right, owners):
        block = stats.shape[-1]
        rows = left.shape[0]
        count = block // 128
        upper = (len(tile_list(count, True)) * 128) % (16 * n_dp) == 0
        tiles = tile_list(count, upper)
        size = len(tiles) * 128
        hbm = pl.BlockSpec(memory_space=pl.ANY)
        vmem = pl.BlockSpec(memory_space=pltpu.VMEM)
        dma = pltpu.SemaphoreType.DMA
        shapes = (
            jax.ShapeDtypeStruct((rows, block), BF16),
            jax.ShapeDtypeStruct((block, block), F32),
            jax.ShapeDtypeStruct((rows, block), BF16),
        )
        results = pl.pallas_call(
            functools.partial(kernel, n_dp, n_f, rows * block * n_f, tiles, upper),
            out_shape=shapes,
            in_specs=[pl.BlockSpec(memory_space=pltpu.HBM)] * 5,
            out_specs=(vmem, vmem, vmem),
            scratch_shapes=[
                pltpu.SMEM((2, n_f), jnp.int32),
                pltpu.VMEM((rows, block), BF16),
                pltpu.VMEM((block, block), F32),
                pltpu.VMEM((rows, block), BF16),
                pltpu.VMEM((block, block), BF16),
                pltpu.VMEM((2 * size, 128), BF16),
                pltpu.VMEM((2, block, block), BF16),
                pltpu.VMEM((2, block, block), BF16),
                pltpu.VMEM((rows, block), BF16),
                pltpu.VMEM((2, size, 128), BF16),
                pltpu.VMEM((2, size, 128), BF16),
                pltpu.VMEM((size, 128), BF16),
                pltpu.VMEM((block, block), BF16),
                pltpu.VMEM((rows, block), BF16),
                pltpu.VMEM((block, block), F32),
                pltpu.VMEM((2 * n_f, 8, 128), F32),
                dma((5,)),
                dma((4, bits)),
                dma((4, bits)),
                dma((4, bits)),
                dma((4, bits)),
                dma((4,)),
                dma((4,)),
                dma((2 * n_f - 1,)),
                dma((2 * n_f - 1,)),
            ],
            compiler_params=pltpu.CompilerParams(
                collective_id=0, has_side_effects=True, vmem_limit_bytes=50 << 20
            ),
        )(owners.T, grads, stats, left, right)
        update, new_stats, new_root = pl.pallas_call(
            write_out,
            out_shape=shapes,
            in_specs=[hbm] * 3,
            out_specs=(hbm, hbm, hbm),
            scratch_shapes=[dma((3,))],
            compiler_params=pltpu.CompilerParams(vmem_limit_bytes=50 << 20),
        )(*results)
        return update, new_stats[None, None], new_root

    in_specs = (
        P("dp", None, "fsdp"),
        P("dp", "fsdp", None, None),
        P(None, "fsdp"),
        P(None, "fsdp"),
        P(),
    )
    out_specs = (P(None, "fsdp"), P("dp", "fsdp", None, None), P(None, "fsdp"))
    return jax.shard_map(local, mesh=mesh, in_specs=in_specs, out_specs=out_specs, check_vma=False)
```

time: 33.9 us -> 34.7 us (1.024)
  Pallas kernels: 32.4 us -> 33.2 us
    pallas_call x1, Pallas kernels: 30.7 us -> 31.5 us  [local(): pl.pallas_call(functools.partial(kernel, n_dp, n_f, rows * block * n_f, t...]
where the time goes in v3:
time: 34.7 us; the launch traced here: 34.5 us
  Pallas kernels  33.2 us (96%)
  local copies, waits for them, and re-layouts  0.67 us (2%)
  between operations  0.65 us (2%)
    pallas_call x1, Pallas kernels, local(): pl.pallas_call(functools.partial(kernel, n_dp, n_f, rows * block * n_f, t...  31.5 us
    pallas_call x1, Pallas kernels, local(): pl.pallas_call(write_out, out_shape=shapes, in_specs=[hbm] * 3, out_specs...  1.69 us

profile of v3, /device:TPU:0, one launch (start us, length us, event | category | flops | bytes accessed | tf_op | source)
XLA Modules:
  0.0 34.5 jit_solution(963127873344901321)
XLA Ops:
  0.6 0.0 copy-start
  0.6 0.7 %copy-done = s32[4,2]{0,1:T(2,128)S(1)} copy-done((s32[4,2]{0,1:T(2,128)S(1)}, s32[4,2]{0,1:T(2,128)}, u32[]{:S(2)}) %copy-start) | copy-done | bytes 56
  1.3 31.5 %shard_map.76 = (bf16[1024,512]{1,0:T(8,128)(2,1)S(1)}, f32[512,512]{1,0:T(8,128)S(1)}, bf16[1024,512]{1,0:T(8,128)(2,1)S(1)}) custom-call(s32[2,4]{1,0:T(2,128)S(1)} %bitcast.2, bf16[1,1024,512]{2,1,0:T(8,128)(2,1)} %grads.1, f32[1,1,512,512]{3,2,1,0:T(8,128)} %stats.1, bf16[1024,512]{1,0:T(8,128)(2,1)} %left.1, bf16[1024,512]{1,0:T(8,128)(2,1)} %right.1), custom_call_target="tpu_custom_call" | custom-call | tf_op jit(solution)/shard_map/pallas_call | solution.py:323
  32.9 1.7 %shard_map.77 = (bf16[1024,512]{1,0:T(8,128)(2,1)}, f32[512,512]{1,0:T(8,128)}, bf16[1024,512]{1,0:T(8,128)(2,1)}) custom-call(bf16[1024,512]{1,0:T(8,128)(2,1)S(1)} %get-tuple-element.9.refs_0_, f32[512,512]{1,0:T(8,128)S(1)} %get-tuple-element.10.refs_1_, bf16[1024,512]{1,0:T(8,128)(2,1)S(1)} %get-tuple-element.11.refs_2_), custom_call_target="tpu_custom_call" | custom-call | tf_op jit(solution)/shard_map/pallas_call | solution.py:359
Async XLA Ops:
  0.6 0.7 %copy-start = (s32[4,2]{0,1:T(2,128)S(1)}, s32[4,2]{0,1:T(2,128)}, u32[]{:S(2)}) copy-start(s32[4,2]{0,1:T(2,128)} %param.9) | copy-start | bytes 100

commit v4 on v3

--- a/solution.py
+++ b/solution.py
@@ -30,10 +30,10 @@
         self.rs_send, self.rs_recv, self.ag_send, self.ag_recv = sems
         self.bit = [(me // (1 << b)) % 2 for b in order]
         self.peer = [me + (1 - 2 * v) * (1 << b) for v, b in zip(self.bit, order)]
-        self.half = [size >> j for j in range(self.n)]
+        self.half = [size >> min(j, max(self.n - 2, 0)) for j in range(self.n)]
         self.at = [0] + [2 * size - (size >> (j - 1)) for j in range(1, self.n)]
         self.low = [base]
-        for j in range(1, self.n):
+        for j in range(1, self.n - 1):
             self.low.append(self.low[-1] + self.bit[j] * self.half[j])
         self.pending = []
 
@@ -53,12 +53,15 @@
         self.pending.append(move)
         return move
 
+    def skip(self, j, v):
+        return 0 if j == self.n - 1 else v * self.half[j]
+
     def start_sum(self, j):
         half = self.half[j]
         if j == 0:
             src = self.source.at[self.rows(self.away, half)]
         else:
-            src = self.part.at[self.rows(self.at[j - 1] + (1 - self.bit[j]) * half, half)]
+            src = self.part.at[self.rows(self.at[j - 1] + self.skip(j, 1 - self.bit[j]), half)]
         self.move = self.copy(
             src,
             self.recv.at[pl.ds(self.at[j], half)],
@@ -71,7 +74,7 @@
         if j == 0:
             mine = self.kept[self.rows(self.near + offset, size), :]
         else:
-            near = self.at[j - 1] + self.bit[j] * self.half[j]
+            near = self.at[j - 1] + self.skip(j, self.bit[j])
             mine = self.part[self.rows(near + offset, size), :]
         other = self.recv[self.rows(self.at[j] + offset, size), :]
         return (mine.astype(F32) + other.astype(F32)).astype(BF16)
@@ -79,9 +82,13 @@
     def end_sum(self, j):
         self.move.wait_recv()
         if j == self.n - 1:
-            self.whole[self.rows(self.low[j], self.half[j]), :] = self.added(j, 0, self.half[j])
-            if j > 0:
-                self.start_spread(j)
+            self.whole[self.rows(self.low[-1], self.half[j]), :] = self.added(j, 0, self.half[j])
+            if j > 1:
+                self.start_spread(j - 1)
+            return
+        if j == self.n - 2:
+            self.part[self.rows(self.at[j], self.half[j]), :] = self.added(j, 0, self.half[j])
+            self.start_sum(j + 1)
             return
         quarter = self.half[j + 1]
         v = self.bit[j + 1]
@@ -219,7 +226,7 @@
     for j in range(1, bits):
         for s in streams:
             s.end_sum(j)
-    for j in range(bits - 1, 0, -1):
+    for j in range(bits - 2, 0, -1):
         for s in of_g:
             s.end_spread(j)
         if j > 1:
@@ -251,6 +258,23 @@
         z_moves.append(move)
     h = mm(q, g).astype(BF16)
     extra[...] = (1.0 - BETA) * mm_t(h, h)
+    if bits > 2:
+        for s in of_a:
+            s.end_spread(1)
+    for k, (r, c) in enumerate(tiles):
+        down, along = pl.ds(r * 128, 128), pl.ds(c * 128, 128)
+        middle = BETA * whole_a[pl.ds(k * 128, 128), :].astype(F32) + extra[down, along]
+        middle = middle.astype(BF16)
+        full[down, along] = middle
+        if upper and r != c:
+            full[along, down] = middle.T
+    middle = full[...]
+    share = block // 4
+    for k in range(4):
+        rows = pl.ds(pl.multiple_of(core * block + k * share, share), share)
+        some = v_left[rows, :]
+        new_root[rows, :] = (1.25 * some.astype(F32) - 0.25 * mm(some, middle)).astype(BF16)
+        swap(new_root.at[rows], new_root.at[rows])
     swaps[0].wait_recv()
     own_g = owned(whole_g)
     has = owns[0] + owns[1]
@@ -264,23 +288,6 @@
     scale = lax.rsqrt(total / entries + EPSILON)
     swaps[1].wait_recv()
     update[...] = (rounded[...].astype(F32) * scale).astype(BF16)
-    if bits > 1:
-        for s in of_a:
-            s.end_spread(1)
-    for k, (r, c) in enumerate(tiles):
-        down, along = pl.ds(r * 128, 128), pl.ds(c * 128, 128)
-        middle = BETA * whole_a[pl.ds(k * 128, 128), :].astype(F32) + extra[down, along]
-        middle = middle.astype(BF16)
-        full[down, along] = middle
-        if upper and r != c:
-            full[along, down] = middle.T
-    middle = full[...]
-    share = block // 2
-    for k in range(2):
-        rows = pl.ds(pl.multiple_of(core * block + k * share, share), share)
-        some = v_left[rows, :]
-        new_root[rows, :] = (1.25 * some.astype(F32) - 0.25 * mm(some, middle)).astype(BF16)
-        swap(new_root.at[rows], new_root.at[rows])
     for move in swaps[2:]:
         move.wait_recv()
     for s in streams:
@@ -347,8 +354,8 @@
                 dma((4, bits)),
                 dma((4, bits)),
                 dma((4, bits)),
-                dma((4,)),
-                dma((4,)),
+                dma((6,)),
+                dma((6,)),
                 dma((2 * n_f - 1,)),
                 dma((2 * n_f - 1,)),
             ],

time: 34.7 us -> 31.4 us (0.905)
  Pallas kernels: 33.2 us -> 29.9 us
    pallas_call x1, Pallas kernels: 31.5 us -> 28.2 us  [local(): pl.pallas_call(functools.partial(kernel, n_dp, n_f, rows * block * n_f, t...]
where the time goes in v4:
time: 31.4 us; the launch traced here: 31.3 us
  Pallas kernels  29.9 us (95%)
  local copies, waits for them, and re-layouts  0.67 us (2%)
  between operations  0.65 us (2%)
    pallas_call x1, Pallas kernels, local(): pl.pallas_call(functools.partial(kernel, n_dp, n_f, rows * block * n_f, t...  28.2 us
    pallas_call x1, Pallas kernels, local(): pl.pallas_call(write_out, out_shape=shapes, in_specs=[hbm] * 3, out_specs...  1.69 us
    unnamed x2, local copies, waits for them, and re-layouts  0.67 us

profile of v4, /device:TPU:0, one launch (start us, length us, event | category | flops | bytes accessed | tf_op | source)
XLA Modules:
  0.0 31.3 jit_solution(6570594914086341925)
XLA Ops:
  0.6 0.0 copy-start
  0.6 0.7 %copy-done = s32[4,2]{0,1:T(2,128)S(1)} copy-done((s32[4,2]{0,1:T(2,128)S(1)}, s32[4,2]{0,1:T(2,128)}, u32[]{:S(2)}) %copy-start) | copy-done | bytes 56
  1.3 28.2 %shard_map.76 = (bf16[1024,512]{1,0:T(8,128)(2,1)S(1)}, f32[512,512]{1,0:T(8,128)S(1)}, bf16[1024,512]{1,0:T(8,128)(2,1)S(1)}) custom-call(s32[2,4]{1,0:T(2,128)S(1)} %bitcast.2, bf16[1,1024,512]{2,1,0:T(8,128)(2,1)} %grads.1, f32[1,1,512,512]{3,2,1,0:T(8,128)} %stats.1, bf16[1024,512]{1,0:T(8,128)(2,1)} %left.1, bf16[1024,512]{1,0:T(8,128)(2,1)} %right.1), custom_call_target="tpu_custom_call" | custom-call | tf_op jit(solution)/shard_map/pallas_call | solution.py:330
  29.6 1.7 %shard_map.77 = (bf16[1024,512]{1,0:T(8,128)(2,1)}, f32[512,512]{1,0:T(8,128)}, bf16[1024,512]{1,0:T(8,128)(2,1)}) custom-call(bf16[1024,512]{1,0:T(8,128)(2,1)S(1)} %get-tuple-element.9.refs_0_, f32[512,512]{1,0:T(8,128)S(1)} %get-tuple-element.10.refs_1_, bf16[1024,512]{1,0:T(8,128)(2,1)S(1)} %get-tuple-element.11.refs_2_), custom_call_target="tpu_custom_call" | custom-call | tf_op jit(solution)/shard_map/pallas_call | solution.py:366
Async XLA Ops:
  0.6 0.7 %copy-start = (s32[4,2]{0,1:T(2,128)S(1)}, s32[4,2]{0,1:T(2,128)}, u32[]{:S(2)}) copy-start(s32[4,2]{0,1:T(2,128)} %param.9) | copy-start | bytes 100

commit v5 on v4

--- a/solution.py
+++ b/solution.py
@@ -159,9 +159,9 @@
     forward = list(range(bits))
     turned = [0] + forward[:0:-1]
     of_g, of_a = [], []
-    for k in range(2):
-        order = forward if k == 0 else turned
-        share = block // 2
+    for k in range(recv_g.shape[0]):
+        order = forward if k % 2 == 0 else turned
+        share = block // recv_g.shape[0]
         of_g.append(
             Stream(
                 me, order, share, grads.at[0], v_grads,
@@ -170,13 +170,16 @@
                 (rs_send.at[k], rs_recv.at[k], ag_send.at[k], ag_recv.at[k]),
             )
         )
+    for k in range(2):
+        order = forward if k == 0 else turned
         share = size // 2
+        e = len(of_g) + k
         of_a.append(
             Stream(
                 me, order, share, masked, masked,
                 core * size + k * share, (1 - core) * size + k * share,
                 recv_a.at[k], part_a.at[k], whole_a, k * share,
-                (rs_send.at[2 + k], rs_recv.at[2 + k], ag_send.at[2 + k], ag_recv.at[2 + k]),
+                (rs_send.at[e], rs_recv.at[e], ag_send.at[e], ag_recv.at[e]),
             )
         )
     streams = of_g + of_a
@@ -298,10 +301,13 @@
 
 def write_out(*refs):
     sources, targets, sems = refs[:3], refs[3:6], refs[6]
-    moves = [
-        pltpu.make_async_copy(src, dst, sems.at[i])
-        for i, (src, dst) in enumerate(zip(sources, targets))
-    ]
+    pieces = sems.shape[1]
+    moves = []
+    for i, (src, dst) in enumerate(zip(sources, targets)):
+        share = src.shape[0] // pieces
+        for k in range(pieces):
+            rows = pl.ds(k * share, share)
+            moves.append(pltpu.make_async_copy(src.at[rows], dst.at[rows], sems.at[i, k]))
     for move in moves:
         move.start()
     for move in moves:
@@ -319,6 +325,7 @@
         upper = (len(tile_list(count, True)) * 128) % (16 * n_dp) == 0
         tiles = tile_list(count, upper)
         size = len(tiles) * 128
+        parts = 4 if block % (32 * n_dp) == 0 else 2
         hbm = pl.BlockSpec(memory_space=pl.ANY)
         vmem = pl.BlockSpec(memory_space=pltpu.VMEM)
         dma = pltpu.SemaphoreType.DMA
@@ -339,8 +346,8 @@
                 pltpu.VMEM((rows, block), BF16),
                 pltpu.VMEM((block, block), BF16),
                 pltpu.VMEM((2 * size, 128), BF16),
-                pltpu.VMEM((2, block, block), BF16),
-                pltpu.VMEM((2, block, block), BF16),
+                pltpu.VMEM((parts, 2 * block // parts, block), BF16),
+                pltpu.VMEM((parts, 2 * block // parts, block), BF16),
                 pltpu.VMEM((rows, block), BF16),
                 pltpu.VMEM((2, size, 128), BF16),
                 pltpu.VMEM((2, size, 128), BF16),
@@ -350,10 +357,10 @@
                 pltpu.VMEM((block, block), F32),
                 pltpu.VMEM((2 * n_f, 8, 128), F32),
                 dma((5,)),
-                dma((4, bits)),
-                dma((4, bits)),
-                dma((4, bits)),
-                dma((4, bits)),
+                dma((parts + 2, bits)),
+                dma((parts + 2, bits)),
+                dma((parts + 2, bits)),
+                dma((parts + 2, bits)),
                 dma((6,)),
                 dma((6,)),
                 dma((2 * n_f - 1,)),
@@ -368,7 +375,7 @@
             out_shape=shapes,
             in_specs=[hbm] * 3,
             out_specs=(hbm, hbm, hbm),
-            scratch_shapes=[dma((3,))],
+            scratch_shapes=[dma((3, 4))],
             compiler_params=pltpu.CompilerParams(vmem_limit_bytes=50 << 20),
         )(*results)
         return update, new_stats[None, None], new_root

time: 31.4 us -> 29.9 us (0.952)
  Pallas kernels: 29.9 us -> 28.4 us
    pallas_call x1, Pallas kernels: 28.2 us -> 26.6 us  [local(): pl.pallas_call(functools.partial(kernel, n_dp, n_f, rows * block * n_f, t...]
where the time goes in v5:
time: 29.9 us; the launch traced here: 29.7 us
  Pallas kernels  28.4 us (95%)
  local copies, waits for them, and re-layouts  0.67 us (2%)
  between operations  0.65 us (2%)
    pallas_call x1, Pallas kernels, local(): pl.pallas_call(functools.partial(kernel, n_dp, n_f, rows * block * n_f, t...  26.6 us
    pallas_call x1, Pallas kernels, local(): pl.pallas_call(write_out, out_shape=shapes, in_specs=[hbm] * 3, out_specs...  1.76 us
    unnamed x2, local copies, waits for them, and re-layouts  0.67 us

profile of v5, /device:TPU:0, one launch (start us, length us, event | category | flops | bytes accessed | tf_op | source)
XLA Modules:
  0.0 29.7 jit_solution(1440651491999626291)
XLA Ops:
  0.6 0.0 copy-start
  0.6 0.7 %copy-done = s32[4,2]{0,1:T(2,128)S(1)} copy-done((s32[4,2]{0,1:T(2,128)S(1)}, s32[4,2]{0,1:T(2,128)}, u32[]{:S(2)}) %copy-start) | copy-done | bytes 56
  1.3 26.6 %shard_map.76 = (bf16[1024,512]{1,0:T(8,128)(2,1)S(1)}, f32[512,512]{1,0:T(8,128)S(1)}, bf16[1024,512]{1,0:T(8,128)(2,1)S(1)}) custom-call(s32[2,4]{1,0:T(2,128)S(1)} %bitcast.2, bf16[1,1024,512]{2,1,0:T(8,128)(2,1)} %grads.1, f32[1,1,512,512]{3,2,1,0:T(8,128)} %stats.1, bf16[1024,512]{1,0:T(8,128)(2,1)} %left.1, bf16[1024,512]{1,0:T(8,128)(2,1)} %right.1), custom_call_target="tpu_custom_call" | custom-call | tf_op jit(solution)/shard_map/pallas_call | solution.py:337
  27.9 1.8 %shard_map.77 = (bf16[1024,512]{1,0:T(8,128)(2,1)}, f32[512,512]{1,0:T(8,128)}, bf16[1024,512]{1,0:T(8,128)(2,1)}) custom-call(bf16[1024,512]{1,0:T(8,128)(2,1)S(1)} %get-tuple-element.9.refs_0_, f32[512,512]{1,0:T(8,128)S(1)} %get-tuple-element.10.refs_1_, bf16[1024,512]{1,0:T(8,128)(2,1)S(1)} %get-tuple-element.11.refs_2_), custom_call_target="tpu_custom_call" | custom-call | tf_op jit(solution)/shard_map/pallas_call | solution.py:373
Async XLA Ops:
  0.6 0.7 %copy-start = (s32[4,2]{0,1:T(2,128)S(1)}, s32[4,2]{0,1:T(2,128)}, u32[]{:S(2)}) copy-start(s32[4,2]{0,1:T(2,128)} %param.9) | copy-start | bytes 100

commit v6 on v5

--- a/solution.py
+++ b/solution.py
@@ -138,7 +138,7 @@
     for i, (src, dst) in enumerate(
         (
             (owners_hbm, owners), (stats.at[0, 0], v_stats), (left, v_left),
-            (grads.at[0], v_grads), (right.at[here], v_right),
+            (grads.at[0, here], v_grads), (right.at[here], v_right),
         )
     ):
         load = pltpu.make_async_copy(src, dst, local_sem.at[i])
@@ -165,14 +165,14 @@
         of_g.append(
             Stream(
                 me, order, share, grads.at[0], v_grads,
-                core * block + k * share, (1 - core) * block + k * share,
+                k * share, (1 - core) * block + k * share,
                 recv_g.at[k], part_g.at[k], whole_g, core * block + k * share,
                 (rs_send.at[k], rs_recv.at[k], ag_send.at[k], ag_recv.at[k]),
             )
         )
-    for k in range(2):
-        order = forward if k == 0 else turned
-        share = size // 2
+    for k in range(recv_a.shape[0]):
+        order = forward if k % 2 == 0 else turned
+        share = size // recv_a.shape[0]
         e = len(of_g) + k
         of_a.append(
             Stream(
@@ -209,9 +209,11 @@
 
     own_x = owned(v_left)
     own_q = mm(own_x, own_x).astype(BF16)
+    loads[3].wait()
+    for s in of_g[:2]:
+        s.end_sum(0)
     own_t = mm(own_q, v_stats[...].astype(BF16)).astype(BF16)
-    loads[3].wait()
-    for s in of_g:
+    for s in of_g[2:]:
         s.end_sum(0)
     own_a = mm(own_t, own_q)
     for i in range(2):
@@ -261,16 +263,20 @@
         z_moves.append(move)
     h = mm(q, g).astype(BF16)
     extra[...] = (1.0 - BETA) * mm_t(h, h)
-    if bits > 2:
-        for s in of_a:
+    done = 0
+    for i, s in enumerate(of_a):
+        if bits > 2:
             s.end_spread(1)
-    for k, (r, c) in enumerate(tiles):
-        down, along = pl.ds(r * 128, 128), pl.ds(c * 128, 128)
-        middle = BETA * whole_a[pl.ds(k * 128, 128), :].astype(F32) + extra[down, along]
-        middle = middle.astype(BF16)
-        full[down, along] = middle
-        if upper and r != c:
-            full[along, down] = middle.T
+        ready = (i + 1) * s.size // 128
+        for k in range(done, ready):
+            r, c = tiles[k]
+            down, along = pl.ds(r * 128, 128), pl.ds(c * 128, 128)
+            middle = BETA * whole_a[pl.ds(k * 128, 128), :].astype(F32) + extra[down, along]
+            middle = middle.astype(BF16)
+            full[down, along] = middle
+            if upper and r != c:
+                full[along, down] = middle.T
+        done = ready
     middle = full[...]
     share = block // 4
     for k in range(4):
@@ -325,6 +331,7 @@
         upper = (len(tile_list(count, True)) * 128) % (16 * n_dp) == 0
         tiles = tile_list(count, upper)
         size = len(tiles) * 128
+        pieces = 4 if size % (32 * n_dp) == 0 else 2
         parts = 4 if block % (32 * n_dp) == 0 else 2
         hbm = pl.BlockSpec(memory_space=pl.ANY)
         vmem = pl.BlockSpec(memory_space=pltpu.VMEM)
@@ -341,7 +348,7 @@
             out_specs=(vmem, vmem, vmem),
             scratch_shapes=[
                 pltpu.SMEM((2, n_f), jnp.int32),
-                pltpu.VMEM((rows, block), BF16),
+                pltpu.VMEM((block, block), BF16),
                 pltpu.VMEM((block, block), F32),
                 pltpu.VMEM((rows, block), BF16),
                 pltpu.VMEM((block, block), BF16),
@@ -349,18 +356,18 @@
                 pltpu.VMEM((parts, 2 * block // parts, block), BF16),
                 pltpu.VMEM((parts, 2 * block // parts, block), BF16),
                 pltpu.VMEM((rows, block), BF16),
-                pltpu.VMEM((2, size, 128), BF16),
-                pltpu.VMEM((2, size, 128), BF16),
+                pltpu.VMEM((pieces, 2 * size // pieces, 128), BF16),
+                pltpu.VMEM((pieces, 2 * size // pieces, 128), BF16),
                 pltpu.VMEM((size, 128), BF16),
                 pltpu.VMEM((block, block), BF16),
                 pltpu.VMEM((rows, block), BF16),
                 pltpu.VMEM((block, block), F32),
                 pltpu.VMEM((2 * n_f, 8, 128), F32),
                 dma((5,)),
-                dma((parts + 2, bits)),
-                dma((parts + 2, bits)),
-                dma((parts + 2, bits)),
-                dma((parts + 2, bits)),
+                dma((parts + pieces, bits)),
+                dma((parts + pieces, bits)),
+                dma((parts + pieces, bits)),
+                dma((parts + pieces, bits)),
                 dma((6,)),
                 dma((6,)),
                 dma((2 * n_f - 1,)),

time: 29.9 us -> 30 us (level)
  no operation moved by 1% of the time
where the time goes in v6:
time: 30 us; the launch traced here: 29.8 us
  Pallas kernels  28.5 us (95%)
  local copies, waits for them, and re-layouts  0.67 us (2%)
  between operations  0.65 us (2%)
    pallas_call x1, Pallas kernels, local(): pl.pallas_call(functools.partial(kernel, n_dp, n_f, rows * block * n_f, t...  26.7 us
    pallas_call x1, Pallas kernels, local(): pl.pallas_call(write_out, out_shape=shapes, in_specs=[hbm] * 3, out_specs...  1.76 us
    unnamed x2, local copies, waits for them, and re-layouts  0.67 us

profile of v6, /device:TPU:0, one launch (start us, length us, event | category | flops | bytes accessed | tf_op | source)
XLA Modules:
  0.0 29.8 jit_solution(17375990269311605235)
XLA Ops:
  0.6 0.0 copy-start
  0.6 0.7 %copy-done = s32[4,2]{0,1:T(2,128)S(1)} copy-done((s32[4,2]{0,1:T(2,128)S(1)}, s32[4,2]{0,1:T(2,128)}, u32[]{:S(2)}) %copy-start) | copy-done | bytes 56
  1.3 26.7 %shard_map.76 = (bf16[1024,512]{1,0:T(8,128)(2,1)S(1)}, f32[512,512]{1,0:T(8,128)S(1)}, bf16[1024,512]{1,0:T(8,128)(2,1)S(1)}) custom-call(s32[2,4]{1,0:T(2,128)S(1)} %bitcast.2, bf16[1,1024,512]{2,1,0:T(8,128)(2,1)} %grads.1, f32[1,1,512,512]{3,2,1,0:T(8,128)} %stats.1, bf16[1024,512]{1,0:T(8,128)(2,1)} %left.1, bf16[1024,512]{1,0:T(8,128)(2,1)} %right.1), custom_call_target="tpu_custom_call" | custom-call | tf_op jit(solution)/shard_map/pallas_call | solution.py:344
  28.1 1.8 %shard_map.77 = (bf16[1024,512]{1,0:T(8,128)(2,1)}, f32[512,512]{1,0:T(8,128)}, bf16[1024,512]{1,0:T(8,128)(2,1)}) custom-call(bf16[1024,512]{1,0:T(8,128)(2,1)S(1)} %get-tuple-element.9.refs_0_, f32[512,512]{1,0:T(8,128)S(1)} %get-tuple-element.10.refs_1_, bf16[1024,512]{1,0:T(8,128)(2,1)S(1)} %get-tuple-element.11.refs_2_), custom_call_target="tpu_custom_call" | custom-call | tf_op jit(solution)/shard_map/pallas_call | solution.py:380
Async XLA Ops:
  0.6 0.7 %copy-start = (s32[4,2]{0,1:T(2,128)S(1)}, s32[4,2]{0,1:T(2,128)}, u32[]{:S(2)}) copy-start(s32[4,2]{0,1:T(2,128)} %param.9) | copy-start | bytes 100

commit v7 on v6

--- a/solution.py
+++ b/solution.py
@@ -331,7 +331,7 @@
         upper = (len(tile_list(count, True)) * 128) % (16 * n_dp) == 0
         tiles = tile_list(count, upper)
         size = len(tiles) * 128
-        pieces = 4 if size % (32 * n_dp) == 0 else 2
+        pieces = 2
         parts = 4 if block % (32 * n_dp) == 0 else 2
         hbm = pl.BlockSpec(memory_space=pl.ANY)
         vmem = pl.BlockSpec(memory_space=pltpu.VMEM)

time: 30 us -> 30 us (level)
  no operation moved by 1% of the time
where the time goes in v7:
time: 30 us; the launch traced here: 29.8 us
  Pallas kernels  28.5 us (95%)
  local copies, waits for them, and re-layouts  0.67 us (2%)
  between operations  0.65 us (2%)
    pallas_call x1, Pallas kernels, local(): pl.pallas_call(functools.partial(kernel, n_dp, n_f, rows * block * n_f, t...  26.7 us
    pallas_call x1, Pallas kernels, local(): pl.pallas_call(write_out, out_shape=shapes, in_specs=[hbm] * 3, out_specs...  1.76 us
    unnamed x2, local copies, waits for them, and re-layouts  0.67 us

profile of v7, /device:TPU:0, one launch (start us, length us, event | category | flops | bytes accessed | tf_op | source)
XLA Modules:
  0.0 29.8 jit_solution(2364849760758969914)
XLA Ops:
  0.6 0.0 copy-start
  0.6 0.7 %copy-done = s32[4,2]{0,1:T(2,128)S(1)} copy-done((s32[4,2]{0,1:T(2,128)S(1)}, s32[4,2]{0,1:T(2,128)}, u32[]{:S(2)}) %copy-start) | copy-done | bytes 56
  1.3 26.7 %shard_map.76 = (bf16[1024,512]{1,0:T(8,128)(2,1)S(1)}, f32[512,512]{1,0:T(8,128)S(1)}, bf16[1024,512]{1,0:T(8,128)(2,1)S(1)}) custom-call(s32[2,4]{1,0:T(2,128)S(1)} %bitcast.2, bf16[1,1024,512]{2,1,0:T(8,128)(2,1)} %grads.1, f32[1,1,512,512]{3,2,1,0:T(8,128)} %stats.1, bf16[1024,512]{1,0:T(8,128)(2,1)} %left.1, bf16[1024,512]{1,0:T(8,128)(2,1)} %right.1), custom_call_target="tpu_custom_call" | custom-call | tf_op jit(solution)/shard_map/pallas_call | solution.py:344
  28.1 1.8 %shard_map.77 = (bf16[1024,512]{1,0:T(8,128)(2,1)}, f32[512,512]{1,0:T(8,128)}, bf16[1024,512]{1,0:T(8,128)(2,1)}) custom-call(bf16[1024,512]{1,0:T(8,128)(2,1)S(1)} %get-tuple-element.9.refs_0_, f32[512,512]{1,0:T(8,128)S(1)} %get-tuple-element.10.refs_1_, bf16[1024,512]{1,0:T(8,128)(2,1)S(1)} %get-tuple-element.11.refs_2_), custom_call_target="tpu_custom_call" | custom-call | tf_op jit(solution)/shard_map/pallas_call | solution.py:380
Async XLA Ops:
  0.6 0.7 %copy-start = (s32[4,2]{0,1:T(2,128)S(1)}, s32[4,2]{0,1:T(2,128)}, u32[]{:S(2)}) copy-start(s32[4,2]{0,1:T(2,128)} %param.9) | copy-start | bytes 100
